TPU v7x, 32 devices: a whole 2x2x4 slice. The times are simulated.
32 devices in a mesh: groups: 2 (over x), blk: 16 (over z, y, core).
Axes of the slice: x: 2, y: 2, z: 4, core: 2. Of those that a mesh axis runs over, the one named last changes fastest.
Arguments:
- tokens: bfloat16 [8192, 4096], P(('groups', 'blk')), parts along dimension 0, may hold values from -6 to 6
- expert_ids: int32 [8192, 8], P(('groups', 'blk')), parts along dimension 0, may hold values from 0 to 127, all different within a row; in each aligned block of 256 rows (0 to 255, 256 to 511, ...) at most 32 rows name the same one
- route_prob: float32 [8192, 8], P(('groups', 'blk')), parts along dimension 0, may hold values from 0.05 to 0.6
- gate_up: bfloat16 [2, 6144, 4096], P(None, 'blk'), may hold values from -0.09375 to 0.09375
- block_scale: float32 [2, 48, 32], P(None, 'blk'), may hold values from 0.25 to 3
Outputs:
- slot_hidden: bfloat16 [1024, 6144], P(('groups', 'blk')), parts along dimension 0
There are 2 independent parts, one for each index of `groups`. A program takes and returns all parts, laid end to end along the dimension named above; an argument that names none is the same for every part. Nothing has to cross between parts.
Inputs may be any that keep to these rules, and one draw needn't show every extreme that they name: `expert_ids`: each row names 8 different experts. Within the 256 rows of one device no expert is named more than 32 times, a bound that some block reaches.
All inputs are finite; a program needn't handle non-finite values.
Results may differ from a plain program's by a relative error of at most 0.0058.
Values may be sent and summed in bfloat16 or wider, within the bound.
A program may use at most 192 MiB of HBM per device.

v0:
```python
import jax
import jax.numpy as jnp
from jax import lax
from jax.sharding import PartitionSpec as P

FF = 1536
SPLIT = 4
QB = 128
CAP = 32


def dequantize(gate_up, block_scale):
    expanded = jnp.repeat(jnp.repeat(block_scale, QB, axis=1), QB, axis=2)
    return (gate_up.astype(jnp.float32) * expanded).astype(jnp.bfloat16)


def slot_table(expert_ids, route_prob, count):
    window = jnp.arange(count, dtype=jnp.int32)
    match = expert_ids[:, :, None] == window[None, None, :]
    routed = jnp.any(match, axis=1)
    share = jnp.sum(jnp.where(match, route_prob[:, :, None], jnp.float32(0.0)), axis=1)
    rank = jnp.cumsum(routed.astype(jnp.int32), axis=0) - 1
    positions = jnp.arange(CAP, dtype=jnp.int32)
    chosen = routed[None] & (rank[None] == positions[:, None, None])
    token_iota = jnp.arange(expert_ids.shape[0], dtype=jnp.int32)
    slot_token = jnp.sum(jnp.where(chosen, token_iota[None, :, None], 0), axis=1).T
    slot_share = jnp.sum(jnp.where(chosen, share[None], jnp.float32(0.0)), axis=1).T
    return (slot_token, slot_share)


def local(tokens, expert_ids, route_prob, gate_up, block_scale):
    experts = lax.axis_size("blk") // SPLIT
    slot_token, slot_share = slot_table(expert_ids, route_prob, experts)
    slot_rows = jnp.take(tokens, slot_token, axis=0)
    own_weights = dequantize(gate_up, block_scale)
    outgoing = jnp.repeat(slot_rows, SPLIT, axis=0)
    proj = jnp.einsum(
        "scd,phd->psch",
        lax.all_to_all(outgoing, "blk", split_axis=0, concat_axis=0, tiled=True),
        own_weights,
        preferred_element_type=jnp.float32,
    )
    hidden = jax.nn.silu(proj[0]) * proj[1]
    returned = lax.all_to_all(hidden, "blk", split_axis=0, concat_axis=2, tiled=True)
    activation = returned.reshape(CAP, experts * FF)
    share_columns = jnp.repeat(slot_share.T, FF, axis=1)
    return (share_columns * activation).astype(jnp.bfloat16)


def solution(mesh):
    placed = (
        P(("groups", "blk"), None),
        P(("groups", "blk"), None),
        P(("groups", "blk"), None),
        P(None, "blk", None),
        P(None, "blk", None),
    )
    return jax.shard_map(
        local, mesh=mesh, in_specs=placed, out_specs=P(("groups", "blk"), None), check_vma=False
    )
```

profile of v0, /device:TPU:0, one launch (start us, length us, event | category | flops | bytes accessed | tf_op | source)
XLA Modules:
  0.0 143.2 jit_solution(8250006996085758779)
XLA Ops:
  0.0 0.9 fusion.11
  0.9 1.2 reduce-window.6
  2.1 0.1 slice.18
  2.2 0.1 copy.21
  2.3 0.1 copy.22
  2.4 0.1 add_bitcast_fusion
  2.5 0.2 select_reduce_fusion
  2.7 0.1 reshape.49
  2.8 1.2 gather_fusion
  4.0 0.2 broadcast_select_fusion
  4.2 2.5 %broadcast_in_dim.80 = bf16[4,4,32,4096]{3,2,1,0:T(8,128)(2,1)} broadcast(bf16[4,32,4096]{2,1,0:T(8,128)(2,1)S(1)} %broadcast_select_fusion), dimensions={0,2,3} | broadcast | bytes 5242880 | tf_op jit(solution)/shard_map/broadcast_in_dim | solution.py:36
  6.6 7.4 %all-to-all-start = ((bf16[16,32,4096]{2,1,0:T(8,128)(2,1)}), bf16[16,32,4096]{2,1,0:T(8,128)(2,1)}, u32[]{:S(2)}, u32[]{:S(2)}) async-start(bf16[16,32,4096]{2,1,0:T(8,128)(2,1)} %bitcast.52), calls=%async_computation | async-start | bytes 8388608 | tf_op jit(solution)/shard_map/all_to_all | solution.py:39
  14.1 7.1 %broadcast_in_dim.74 = f32[2,384,32,128]{3,2,1,0:T(8,128)} broadcast(f32[2,384,32]{2,1,0:T(8,128)S(1)} %bitcast.58), dimensions={0,1,2} | broadcast | bytes 12681216 | tf_op jit(solution)/shard_map/broadcast_in_dim | solution.py:13
  21.2 13.8 %reshape.43 = f32[2,384,4096]{2,1,0:T(8,128)} reshape(f32[2,384,32,128]{3,2,1,0:T(8,128)} %broadcast_in_dim.74) | data formatting | bytes 25165824 | tf_op jit(solution)/shard_map/reshape | solution.py:13
  35.0 56.7 %all-to-all-done = bf16[16,32,4096]{2,1,0:T(8,128)(2,1)} async-done(((bf16[16,32,4096]{2,1,0:T(8,128)(2,1)}), bf16[16,32,4096]{2,1,0:T(8,128)(2,1)}, u32[]{:S(2)}, u32[]{:S(2)}) %all-to-all-start) | async-done | bytes 4194336 | tf_op jit(solution)/shard_map/all_to_all | solution.py:39
  91.8 10.0 %fusion.4 = f32[2,16,32,384]{3,2,1,0:T(8,128)S(1)} fusion(bf16[16,32,4096]{2,1,0:T(8,128)(2,1)} %all-to-all-done, f32[2,384,4096]{2,1,0:T(8,128)} %reshape.43, bf16[2,384,4096]{2,1,0:T(8,128)(2,1)} %param.8), kind=kOutput, calls=%fused_computation.5 | convolution fusion | flops 3230662656 | bytes 24641536 | tf_op jit(solution)/shard_map/scd,phd->psch/dot_general | solution.py:37
  101.7 1.1 fusion.9
  102.8 19.6 %all-to-all-start.1 = ((f32[16,32,384]{2,1,0:T(8,128)}), f32[16,32,384]{2,1,0:T(8,128)S(1)}, u32[]{:S(2)}, u32[]{:S(2)}) async-start(f32[16,32,384]{2,1,0:T(8,128)} %fusion.9), calls=%async_computation.1 | async-start | bytes 1572864 | tf_op jit(solution)/shard_map/all_to_all | solution.py:44
  122.5 0.1 select_reduce_fusion.1
  122.6 0.1 copy.23
  122.7 0.2 broadcast_in_dim.72
  122.9 1.1 copy.28
  124.0 17.2 %all-to-all-done.1 = f32[16,32,384]{2,1,0:T(8,128)S(1)} async-done(((f32[16,32,384]{2,1,0:T(8,128)}), f32[16,32,384]{2,1,0:T(8,128)S(1)}, u32[]{:S(2)}, u32[]{:S(2)}) %all-to-all-start.1) | async-done | bytes 786464 | tf_op jit(solution)/shard_map/all_to_all | solution.py:44
  141.3 1.9 %multiply_convert_fusion.1 = bf16[32,6144]{1,0:T(8,128)(2,1)} fusion(f32[32,6144]{1,0:T(8,128)} %bitcast.56, f32[32,6144]{1,0:T(8,128)S(1)} %bitcast.57), kind=kLoop, calls=%fused_computation.10 | loop fusion | flops 393216 | bytes 1966080 | tf_op jit(solution)/shard_map/convert_element_type | solution.py:47
  (20 shorter events, 0.2 us)
Async XLA Ops:
  0.0 2.8 %copy-start = (bf16[256,4096]{1,0:T(8,128)(2,1)S(1)}, bf16[256,4096]{1,0:T(8,128)(2,1)}, u32[]{:S(2)}) copy-start(bf16[256,4096]{1,0:T(8,128)(2,1)} %param.5) | copy-start | bytes 6291460
  4.2 9.9 %copy-start.3 = (f32[2,3,32]{2,0,1:T(2,128)S(1)}, f32[2,3,32]{2,0,1:T(2,128)}, u32[]{:S(2)}) copy-start(f32[2,3,32]{2,0,1:T(2,128)} %param.9) | copy-start | bytes 2308
  6.6 85.1 %all-to-all-start = ((bf16[16,32,4096]{2,1,0:T(8,128)(2,1)}), bf16[16,32,4096]{2,1,0:T(8,128)(2,1)}, u32[]{:S(2)}, u32[]{:S(2)}) async-start(bf16[16,32,4096]{2,1,0:T(8,128)(2,1)} %bitcast.52), calls=%async_computation | async-start | bytes 8388608 | tf_op jit(solution)/shard_map/all_to_all | solution.py:39
  35.0 87.5 %copy-start.1 = (s32[256,8]{0,1:T(8,128)S(1)}, s32[256,8]{0,1:T(8,128)}, u32[]{:S(2)}) copy-start(s32[256,8]{0,1:T(8,128)} %param.6) | copy-start | bytes 24580
  35.0 87.5 %copy-start.2 = (f32[256,8]{0,1:T(8,128)S(1)}, f32[256,8]{0,1:T(8,128)}, u32[]{:S(2)}) copy-start(f32[256,8]{0,1:T(8,128)} %param.7) | copy-start | bytes 24580
  102.8 38.4 %all-to-all-start.1 = ((f32[16,32,384]{2,1,0:T(8,128)}), f32[16,32,384]{2,1,0:T(8,128)S(1)}, u32[]{:S(2)}, u32[]{:S(2)}) async-start(f32[16,32,384]{2,1,0:T(8,128)} %fusion.9), calls=%async_computation.1 | async-start | bytes 1572864 | tf_op jit(solution)/shard_map/all_to_all | solution.py:44
where the time goes:
time: 144 us; the launch traced here: 143 us
  waiting for transfers between devices  73.9 us (51%)
  starting transfers between devices  27.1 us (19%)
  local copies, waits for them, and re-layouts  26.4 us (18%)
  matrix products  9.96 us (7%)
  other arithmetic  5.75 us (4%)
    all_to_all x1, waiting for transfers between devices, local(): lax.all_to_all(outgoing, 'blk', split_axis=0, concat_axis=0, tiled=True)  56.7 us
    all_to_all x1, starting transfers between devices, local(): lax.all_to_all(hidden, 'blk', split_axis=0, concat_axis=2, tiled=True)  19.6 us
    all_to_all x1, waiting for transfers between devices, local(): lax.all_to_all(hidden, 'blk', split_axis=0, concat_axis=2, tiled=True)  17.2 us
    reshape x1, local copies, waits for them, and re-layouts, dequantize(): expanded = jnp.repeat(jnp.repeat(block_scale, QB, axis=1), QB, axis=2)  13.8 us
    dot_general x1, matrix products, local(): jnp.einsum('scd,phd->psch', lax.all_to_all(outgoing, 'blk', split_axis=0,...  9.96 us
    all_to_all x1, starting transfers between devices, local(): lax.all_to_all(outgoing, 'blk', split_axis=0, concat_axis=0, tiled=True)  7.44 us
    broadcast_in_dim x2, local copies, waits for them, and re-layouts, dequantize(): expanded = jnp.repeat(jnp.repeat(block_scale, QB, axis=1), QB, axis=2)  7.12 us
  transfers between devices with their start and end apart: 2, of which 2 were waited for; matrix products, arithmetic and copies ran while one was open for 16% of the time, Pallas kernels for 0%

commit v1 on v0

v1 whole, which is shorter than its diff:
```python
import functools

import jax
import jax.numpy as jnp
from jax import lax
from jax.experimental import pallas as pl
from jax.experimental.pallas import tpu as pltpu
from jax.sharding import PartitionSpec as P

SPLIT = 4
QB = 128
CAP = 32
F32 = jnp.float32
BF16 = jnp.bfloat16


def xor(v, s):
    out, bit = v, 1
    while bit <= s:
        if s & bit:
            out = out + bit - 2 * bit * lax.rem(lax.div(v, bit), 2)
        bit *= 2
    return out


def kernel(n, parts, ids_ref, prob_ref, scale_ref, tok_hbm, w_hbm, out_ref,
           tok, w, tx, rx, hid, ret, share,
           load_sem, z_send, z_recv, y_send, y_recv, a_send, a_recv, b_send, b_recv, r_send, r_recv):
    quads = n // SPLIT
    tokens, depth = tok.shape
    width = depth // parts
    tiles = w.shape[0]
    me = lax.axis_index("blk")
    quad, member = lax.div(me, SPLIT), lax.rem(me, SPLIT)

    def remote(src, dst, send, recv, target):
        copy = pltpu.make_async_remote_copy(
            src_ref=src, dst_ref=dst, send_sem=send, recv_sem=recv,
            device_id={"blk": target}, device_id_type=pl.DeviceIdType.MESH)
        copy.start()
        started.append(copy)
        return copy

    started = []
    load_tokens = pltpu.make_async_copy(tok_hbm, tok, load_sem.at[0])
    load_tokens.start()
    barrier = pltpu.get_barrier_semaphore()
    for step in range(1, n):
        pl.semaphore_signal(barrier, inc=1, device_id={"blk": lax.rem(me + step, n)},
                            device_id_type=pl.DeviceIdType.MESH)
    loads = []
    for t in range(tiles):
        for proj in range(2):
            load = pltpu.make_async_copy(
                w_hbm.at[proj, pl.ds(t * QB, QB)], w.at[t, pl.ds(proj * QB, QB)],
                load_sem.at[1 + 2 * t + proj])
            load.start()
            loads.append(load)

    slots = quads * CAP
    lane = lax.broadcasted_iota(jnp.int32, (tokens, slots), 1)
    expert, place = lane // CAP, lane % CAP
    routed = jnp.zeros((tokens, slots), F32)
    portion = jnp.zeros((tokens, slots), F32)
    for j in range(ids_ref.shape[1]):
        hit = ids_ref[:, j:j + 1] == expert
        routed = jnp.where(hit, F32(1), routed)
        portion = jnp.where(hit, prob_ref[:, j:j + 1], portion)
    earlier = lax.broadcasted_iota(jnp.int32, (tokens, tokens), 1) <= lax.broadcasted_iota(
        jnp.int32, (tokens, tokens), 0)
    count = jnp.dot(jnp.where(earlier, F32(1), F32(0)).astype(BF16), routed.astype(BF16),
                    preferred_element_type=F32)
    chosen = jnp.where(count == (place + 1).astype(F32), routed, F32(0))
    pick = chosen.T.astype(BF16)

    load_tokens.wait()

    def gather(k):
        rows = jnp.dot(pick, tok[:, k * width:(k + 1) * width], preferred_element_type=F32).astype(BF16)
        for e in range(quads):
            tx[e, k] = rows[e * CAP:(e + 1) * CAP]

    def send_z(s, k):
        there = xor(quad, s)
        zs[s, k] = remote(tx.at[there, k], rx.at[me, k], z_send.at[s, k], z_recv.at[s, k],
                          there * SPLIT + member)

    def send_quad(s, k, source):
        block = xor(quad, s) * SPLIT + member
        base = quad * SPLIT
        ys[s, k] = remote(source, rx.at[block, k], y_send.at[s, k], y_recv.at[s, k],
                          base + xor(member, 2))
        near[s, k] = remote(source, rx.at[block, k], a_send.at[s, k], a_recv.at[s, k],
                            base + xor(member, 1))

    def arrived_z(s, k):
        zs[s, k].wait_recv()
        send_quad(s, k, rx.at[xor(quad, s) * SPLIT + member, k])

    def arrived_y(s, k):
        ys[s, k].wait_recv()
        block = xor(quad, s) * SPLIT + xor(member, 2)
        far[s, k] = remote(rx.at[block, k], rx.at[block, k], b_send.at[s, k], b_recv.at[s, k],
                           quad * SPLIT + xor(member, 1))

    def scale_weights(index):
        t, proj = index // 2, index % 2
        loads[index].wait()

        def body(kb, carry):
            where = (t, pl.ds(proj * QB, QB), pl.ds(pl.multiple_of(kb * QB, QB), QB))
            w[where] = (w[where].astype(F32) * scale_ref[proj, t, kb]).astype(BF16)
            return carry

        lax.fori_loop(0, depth // QB, body, 0, unroll=4)

    def compute(s):
        there = xor(quad, s)
        for k in range(parts):
            near[s, k].wait_recv()
            far[s, k].wait_recv()
        first = there * SPLIT

        def body(t, carry):
            x = jnp.concatenate(
                [rx[pl.ds(first, SPLIT), k].reshape(SPLIT * CAP, width) for k in range(parts)], axis=1)
            both = lax.dot_general(x, w[t], (((1,), (1,)), ((), ())), preferred_element_type=F32)
            gate, up = both[:, :QB], both[:, QB:]
            act = (gate / (F32(1) + jnp.exp(-gate)) * up).astype(BF16)
            hid[pl.ds(first, SPLIT), t] = act.reshape(SPLIT, CAP, QB)
            return carry

        lax.fori_loop(0, tiles, body, 0)
        for r in range(SPLIT):
            if s or r:
                target = first + xor(member, r)
                back[s, r] = remote(hid.at[target], ret.at[me], r_send.at[s, r], r_recv.at[s, r], target)

    def finish(s):
        there = xor(quad, s)
        scale = share[pl.ds(pl.multiple_of(there * CAP, CAP), CAP), :]
        for r in range(SPLIT):
            source = there * SPLIT + xor(member, r)
            if s or r:
                back[s, r].wait_recv()
            for t in range(tiles):
                act = ret[source, t] if s or r else hid[source, t]
                at = pl.multiple_of((source * tiles + t) * QB, QB)
                out_ref[:, pl.ds(at, QB)] = (scale * act.astype(F32)).astype(BF16)

    zs, ys, near, far, back = {}, {}, {}, {}, {}
    lead = [quads // 2, 1]
    order = [(s, k) for k in range(parts) for s in lead]
    order += [(s, k) for s in range(1, quads) if s not in lead for k in range(parts)]
    window = 2 * parts

    pl.semaphore_wait(barrier, n - 1)
    for k in range(parts):
        gather(k)
        for s, piece in order[:window]:
            if piece == k:
                send_z(s, k)
        send_quad(0, k, tx.at[quad, k])
    own = pltpu.make_async_copy(tx.at[quad], rx.at[me], load_sem.at[0])
    own.start()
    part_share = jnp.sum((chosen * portion).T, axis=1, keepdims=True)
    share[...] = jnp.broadcast_to(part_share, share.shape)

    todo = [functools.partial(scale_weights, i) for i in range(2 * tiles)]
    for k in range(parts):
        todo.pop(0)()
        arrived_y(0, k)
    own.wait()

    left = {s: parts for s in range(1, quads)}
    ready, done = [0], []
    lag = 2
    behind = []
    for i, (s, k) in enumerate(order):
        arrived_z(s, k)
        if i + window < len(order):
            send_z(*order[i + window])
        behind.append((s, k))
        while todo and i % 2 == 1:
            todo.pop(0)()
            break
        if len(behind) > lag or i == len(order) - 1:
            while len(behind) > (lag if i < len(order) - 1 else 0):
                late = behind.pop(0)
                arrived_y(*late)
                left[late[0]] -= 1
                if left[late[0]] == 0:
                    ready.append(late[0])
        if i == len(order) - 1:
            while todo:
                todo.pop(0)()
        if not todo:
            while ready:
                s_now = ready.pop(0)
                compute(s_now)
                done.append(s_now)
    for s in done:
        finish(s)
    for copy in started:
        copy.wait_send()


def local(n, ids, prob, scale, tokens, gate_up):
    quads = n // SPLIT
    parts = max(2, 16 // quads)
    count, depth = tokens.shape
    tiles = gate_up.shape[1] // QB
    dma = pltpu.SemaphoreType.DMA
    vmem = pl.BlockSpec(memory_space=pltpu.VMEM)
    hbm = pl.BlockSpec(memory_space=pl.ANY)
    return pl.pallas_call(
        functools.partial(kernel, n, parts),
        out_shape=jax.ShapeDtypeStruct((CAP, n * tiles * QB), BF16),
        in_specs=[vmem, vmem, pl.BlockSpec(memory_space=pltpu.SMEM), hbm, hbm],
        out_specs=vmem,
        scratch_shapes=[
            pltpu.VMEM((count, depth), BF16),
            pltpu.VMEM((tiles, 2 * QB, depth), BF16),
            pltpu.VMEM((quads, parts, CAP, depth // parts), BF16),
            pltpu.VMEM((n, parts, CAP, depth // parts), BF16),
            pltpu.VMEM((n, tiles, CAP, QB), BF16),
            pltpu.VMEM((n, tiles, CAP, QB), BF16),
            pltpu.VMEM((quads * CAP, QB), F32),
            dma((1 + 2 * tiles,)),
        ] + [dma((quads, parts))] * 8 + [dma((quads, SPLIT))] * 2,
        compiler_params=pltpu.CompilerParams(
            collective_id=0, has_side_effects=True, vmem_limit_bytes=56 * 1024 * 1024),
        cost_estimate=pl.CostEstimate(
            flops=2 * n * CAP * 2 * tiles * QB * depth, bytes_accessed=10 ** 7, transcendentals=0),
    )(ids, prob, scale, tokens, gate_up)


def solution(mesh):
    n = mesh.shape["blk"]
    placed = (
        P(("groups", "blk"), None),
        P(("groups", "blk"), None),
        P(("groups", "blk"), None),
        P(None, "blk", None),
        P(None, "blk", None),
    )

    def body(tokens, expert_ids, route_prob, gate_up, block_scale):
        return local(n, expert_ids, route_prob, block_scale, tokens, gate_up)

    return jax.shard_map(
        body, mesh=mesh, in_specs=placed, out_specs=P(("groups", "blk"), None), check_vma=False
    )
```

time: 144 us -> 58 us (0.40)
  waiting for transfers between devices: 73.9 us -> 0 us
  Pallas kernels: 0 us -> 51.7 us
  starting transfers between devices: 27.1 us -> 0 us
  local copies, waits for them, and re-layouts: 26.4 us -> 6.01 us
  matrix products: 9.96 us -> 0 us
  other arithmetic: 5.75 us -> 0 us
    all_to_all x2 -> x0, waiting for transfers between devices: 73.9 us -> none  [the longest x1 56.7 us: local(): lax.all_to_all(outgoing, 'blk', split_axis=0, concat_axis=0, tiled=True)]
    pallas_call x0 -> x1, Pallas kernels: none -> 51.7 us  [local(): pl.pallas_call(functools.partial(kernel, n, parts), out_shape=jax.ShapeDt...]
    all_to_all x2 -> x0, starting transfers between devices: 27.1 us -> none  [the longest x1 19.6 us: local(): lax.all_to_all(hidden, 'blk', split_axis=0, concat_axis=2, tiled=True)]
    reshape x1 -> x0, local copies, waits for them, and re-layouts: 13.8 us -> none  [dequantize(): expanded = jnp.repeat(jnp.repeat(block_scale, QB, axis=1), QB, axis=2)]
    dot_general x1 -> x0, matrix products: 9.96 us -> none  [local(): jnp.einsum('scd,phd->psch', lax.all_to_all(outgoing, 'blk', split_axis=0,...]
    broadcast_in_dim x5 -> x0, local copies, waits for them, and re-layouts: 9.83 us -> none  [the longest x2 7.12 us: dequantize(): expanded = jnp.repeat(jnp.repeat(block_scale, QB, axis=1), QB, axis=2)]
    unnamed x12 -> x4, local copies, waits for them, and re-layouts: 1.2 us -> 6.01 us
    convert_element_type x1 -> x0, other arithmetic: 1.95 us -> none  [local(): return (share_columns * activation).astype(jnp.bfloat16)]
  transfers between devices with their start and end apart: 2 -> 0, of which waited for: 2 -> 0; matrix products, arithmetic and copies ran while one was open for 16% -> 0% of each run, Pallas kernels for 0% -> 0%
where the time goes in v1:
time: 58 us; the launch traced here: 57.7 us
  Pallas kernels  51.7 us (89%)
  local copies, waits for them, and re-layouts  6.01 us (10%)
    pallas_call x1, Pallas kernels, local(): pl.pallas_call(functools.partial(kernel, n, parts), out_shape=jax.ShapeDt...  51.7 us
    unnamed x4, local copies, waits for them, and re-layouts  6.01 us

profile of v1, /device:TPU:0, one launch (start us, length us, event | category | flops | bytes accessed | tf_op | source)
XLA Modules:
  0.0 57.7 jit_solution(6663953665204266638)
XLA Ops:
  0.0 1.3 %copy.8.scale_ref = f32[2,3,32]{2,1,0:T(4,128)} copy(f32[2,3,32]{2,0,1:T(2,128)} %param.9) | data formatting | bytes 1536 | tf_op args[4]
  1.3 1.5 %copy.6.ids_ref = s32[256,8]{1,0:T(8,128)} copy(s32[256,8]{0,1:T(8,128)} %param.6) | data formatting | bytes 16384 | tf_op args[1]
  2.8 1.5 %copy.7.prob_ref = f32[256,8]{1,0:T(8,128)} copy(f32[256,8]{0,1:T(8,128)} %param.7) | data formatting | bytes 16384 | tf_op args[2]
  4.2 51.7 %shard_map.55 = bf16[32,6144]{1,0:T(8,128)(2,1)} custom-call(s32[256,8]{1,0:T(8,128)} %copy.6.ids_ref, f32[256,8]{1,0:T(8,128)} %copy.7.prob_ref, f32[2,3,32]{2,1,0:T(4,128)} %copy.8.scale_ref, bf16[256,4096]{1,0:T(8,128)(2,1)} %tok_hbm.1, bf16[2,384,4096]{2,1,0:T(8,128)(2,1)} %w_hbm.1), custom_call_target="tpu_custom_call" | custom-call | flops 3221225472 | bytes 10000000 | tf_op jit(solution)/shard_map/pallas_call | solution.py:216
  55.9 1.8 %copy.10 = bf16[32,6144]{1,0:T(8,128)(2,1)} copy(bf16[32,6144]{1,0:T(8,128)(2,1)} %shard_map.55) | data formatting | bytes 786432

commit v2 on v0

v2 whole, which is shorter than its diff:
```python
import functools

import jax
import jax.numpy as jnp
from jax import lax
from jax.experimental import pallas as pl
from jax.experimental.pallas import tpu as pltpu
from jax.sharding import PartitionSpec as P

SPLIT = 4
QB = 128
CAP = 32
HALF = CAP // 2
WINDOW = 4
LAG = 4
BEFORE = 4
F32 = jnp.float32
BF16 = jnp.bfloat16


def xor(v, s):
    out, bit = v, 1
    while bit <= s:
        if s & bit:
            out = out + bit - 2 * bit * lax.rem(lax.div(v, bit), 2)
        bit *= 2
    return out


def kernel(n, parts, ids_ref, prob_ref, scale_ref, tok_hbm, w_hbm, out_ref,
           tok, w, tx, rx, hid, ret, share, load_sem, sent, z_recv, y_recv, near_recv, far_recv, r_recv):
    quads = n // SPLIT
    tokens, depth = tok.shape
    width = depth // parts
    tiles = w.shape[0]
    me = lax.axis_index("blk")
    quad, member = lax.div(me, SPLIT), lax.rem(me, SPLIT)
    chunks = [(h, c) for h in range(2) for c in range(parts)]

    barrier = pltpu.get_barrier_semaphore()
    for step in range(1, n):
        pl.semaphore_signal(barrier, inc=1, device_id={"blk": lax.rem(me + step, n)},
                            device_id_type=pl.DeviceIdType.MESH)
    load_tokens = pltpu.make_async_copy(tok_hbm, tok, load_sem.at[0])
    load_tokens.start()
    loads = []
    for t in range(tiles):
        for proj in range(2):
            load = pltpu.make_async_copy(
                w_hbm.at[proj, pl.ds(t * QB, QB)], w.at[t, pl.ds(proj * QB, QB)],
                load_sem.at[1 + 2 * t + proj])
            load.start()
            loads.append(load)

    def remote(src, dst, send, recv, target):
        copy = pltpu.make_async_remote_copy(
            src_ref=src, dst_ref=dst, send_sem=send, recv_sem=recv,
            device_id={"blk": target}, device_id_type=pl.DeviceIdType.MESH)
        copy.start()
        return copy

    def wait_for(ref, sem):
        pltpu.make_async_copy(ref, ref, sem).wait()

    slots = quads * CAP
    row = lax.broadcasted_iota(jnp.int32, (slots, tokens), 0)
    expert, place = row // CAP, row % CAP
    routed = jnp.zeros((slots, tokens), F32)
    portion = jnp.zeros((slots, tokens), F32)
    for j in range(ids_ref.shape[0]):
        hit = ids_ref[j:j + 1, :] == expert
        routed = jnp.where(hit, F32(1), routed)
        portion = jnp.where(hit, prob_ref[j:j + 1, :], portion)
    earlier = lax.broadcasted_iota(jnp.int32, (tokens, tokens), 0) <= lax.broadcasted_iota(
        jnp.int32, (tokens, tokens), 1)
    count = jnp.dot(routed.astype(BF16), jnp.where(earlier, F32(1), F32(0)).astype(BF16),
                    preferred_element_type=F32)
    chosen = jnp.where(count == (place + 1).astype(F32), routed, F32(0))
    pick = chosen.astype(BF16)
    total = jnp.sum(chosen * portion, axis=1, keepdims=True)
    share[...] = jnp.broadcast_to(total, share.shape)

    load_tokens.wait()
    for c in range(parts):
        rows = jnp.dot(pick, tok[:, c * width:(c + 1) * width], preferred_element_type=F32).astype(BF16)
        for e in range(quads):
            for h in range(2):
                tx[e, h, c] = rows[e * CAP + h * HALF:e * CAP + (h + 1) * HALF]

    def scale_weights(index):
        t, proj = index // 2, index % 2
        loads[index].wait()

        def body(kb, carry):
            where = (t, pl.ds(proj * QB, QB), pl.ds(pl.multiple_of(kb * QB, QB), QB))
            w[where] = (w[where].astype(F32) * scale_ref[t, proj, kb]).astype(BF16)
            return carry

        lax.fori_loop(0, depth // QB, body, 0, unroll=4)

    zs, ys = {}, {}

    def send_z(s, h, c):
        there = xor(quad, s)
        zs[s, h, c] = remote(tx.at[there, h, c], rx.at[me, h, c], sent.at[0], z_recv.at[s, h, c],
                             there * SPLIT + member)

    def send_quad(s, h, c, source):
        block = xor(quad, s) * SPLIT + member
        base = quad * SPLIT
        ys[s, h, c] = remote(source, rx.at[block, h, c], sent.at[1], y_recv.at[s, h, c],
                             base + xor(member, 2))
        remote(source, rx.at[block, h, c], sent.at[2], near_recv.at[s, h], base + xor(member, 1))

    def arrived_z(s, h, c):
        zs[s, h, c].wait_recv()
        send_quad(s, h, c, rx.at[xor(quad, s) * SPLIT + member, h, c])

    def arrived_y(s, h, c):
        ys[s, h, c].wait_recv()
        block = xor(quad, s) * SPLIT + xor(member, 2)
        remote(rx.at[block, h, c], rx.at[block, h, c], sent.at[3], far_recv.at[s, h],
               quad * SPLIT + xor(member, 1))

    def arrived_all(s, halves):
        for h in halves:
            wait_for(rx.at[0, 0], near_recv.at[s, h])
            wait_for(rx.at[0, 0], far_recv.at[s, h])

    def compute(s, halves, t):
        first = pl.ds(xor(quad, s) * SPLIT, SPLIT)
        which = slice(None) if len(halves) == 2 else halves[0]
        count = SPLIT * HALF * len(halves)
        x = jnp.concatenate([rx[first, which, c].reshape(count, width) for c in range(parts)], axis=1)
        both = lax.dot_general(x, w[t], (((1,), (1,)), ((), ())), preferred_element_type=F32)
        gate, up = both[:, :QB], both[:, QB:]
        act = (gate / (F32(1) + jnp.exp(-gate)) * up).astype(BF16)
        if len(halves) == 2:
            hid[first, :, t] = act.reshape(SPLIT, 2, HALF, QB)
        else:
            hid[first, which, t] = act.reshape(SPLIT, HALF, QB)

    def send_back(s, halves):
        for r in range(SPLIT):
            target = xor(quad, s) * SPLIT + xor(member, r)
            if s == 0 and r == 0:
                continue
            elif len(halves) == 2:
                remote(hid.at[target], ret.at[me], sent.at[4], r_recv.at[s], target)
            else:
                h = halves[0]
                remote(hid.at[target, h], ret.at[me, h], sent.at[4], r_recv.at[s], target)

    def finish(s):
        wait_for(ret.at[pl.ds(0, SPLIT if s else SPLIT - 1)], r_recv.at[s])
        there = xor(quad, s)
        for r in range(SPLIT):
            source = there * SPLIT + xor(member, r)
            back = ret if s or r else hid
            for h in range(2):
                scale = share[pl.ds(pl.multiple_of(there * CAP + h * HALF, HALF), HALF), :]
                for t in range(tiles):
                    at = pl.multiple_of((source * tiles + t) * QB, QB)
                    out_ref[h * HALF:(h + 1) * HALF, pl.ds(at, QB)] = (
                        scale * back[source, h, t].astype(F32)).astype(BF16)

    lead = quads // 2
    last = quads - 1
    rest = [s for s in range(1, last) if s != lead]
    order = []
    for h, c in chunks:
        order += [(lead, h, c), (rest[0], h, c)]
    for s in rest[1:] + [last]:
        order += [(s, h, c) for h, c in chunks]

    todo = [functools.partial(scale_weights, i) for i in range(2 * tiles)]
    for _ in range(BEFORE):
        todo.pop(0)()
    own = pltpu.make_async_copy(tx.at[quad], rx.at[me], load_sem.at[0])
    own.start()

    pl.semaphore_wait(barrier, n - 1)
    local_chunks = list(chunks)
    behind = []

    def local_chunk():
        h, c = local_chunks.pop(0)
        send_quad(0, h, c, tx.at[quad, h, c])
        behind.append((0, h, c))

    for i in range(WINDOW):
        send_z(*order[i])
        if i < 2:
            local_chunk()
    while todo:
        todo.pop(0)()
    own.wait()

    left = {}
    for s in range(quads):
        for h in range(2):
            left[s, h] = parts
    issued = [WINDOW]

    def queue(s, halves):
        todo.append(functools.partial(arrived_all, s, halves))
        if quads <= 4:
            todo.extend(functools.partial(compute, s, halves, t) for t in range(tiles))
        else:
            todo.append(lambda: pl.loop(0, tiles)(functools.partial(compute, s, halves)))
        todo.append(functools.partial(send_back, s, halves))

    def take_y():
        s, h, c = behind.pop(0)
        arrived_y(s, h, c)
        left[s, h] -= 1
        if left[s, h] == 0:
            if s == last:
                queue(s, (h,))
            elif left[s, 1 - h] == 0:
                queue(s, (0, 1))

    for i, event in enumerate(order):
        work = len(todo)
        arrived_z(*event)
        behind.append(event)
        while issued[0] < len(order) and issued[0] <= i + WINDOW:
            send_z(*order[issued[0]])
            issued[0] += 1
        if local_chunks:
            local_chunk()
        while len(behind) > LAG:
            take_y()
        for _ in range(min(work, 3)):
            todo.pop(0)()
    while behind:
        take_y()
        if todo:
            todo.pop(0)()
    while todo:
        todo.pop(0)()
    for s in range(quads):
        finish(s)
    wait_for(tx.at[pl.ds(0, quads - 1)], sent.at[0])
    for kind in (1, 2, 3):
        wait_for(tx, sent.at[kind])
    wait_for(hid.at[pl.ds(0, n - 1)], sent.at[4])


def local(n, ids, prob, scale, tokens, gate_up):
    quads = n // SPLIT
    parts = max(1, 8 // quads)
    count, depth = tokens.shape
    tiles = gate_up.shape[1] // QB
    dma = pltpu.SemaphoreType.DMA
    vmem = pl.BlockSpec(memory_space=pltpu.VMEM)
    hbm = pl.BlockSpec(memory_space=pl.ANY)
    chunk = (2, parts, HALF, depth // parts)
    params = dict(vmem_limit_bytes=56 * 1024 * 1024)
    return pl.pallas_call(
        functools.partial(kernel, n, parts),
        out_shape=jax.ShapeDtypeStruct((CAP, n * tiles * QB), BF16),
        in_specs=[vmem, vmem, pl.BlockSpec(memory_space=pltpu.SMEM), hbm, hbm],
        out_specs=vmem,
        scratch_shapes=[
            pltpu.VMEM((count, depth), BF16),
            pltpu.VMEM((tiles, 2 * QB, depth), BF16),
            pltpu.VMEM((quads,) + chunk, BF16),
            pltpu.VMEM((n,) + chunk, BF16),
            pltpu.VMEM((n, 2, tiles, HALF, QB), BF16),
            pltpu.VMEM((n, 2, tiles, HALF, QB), BF16),
            pltpu.VMEM((quads * CAP, QB), F32),
            dma((1 + 2 * tiles,)),
            dma((5,)),
            dma((quads, 2, parts)),
            dma((quads, 2, parts)),
            dma((quads, 2)),
            dma((quads, 2)),
            dma((quads,)),
        ],
        compiler_params=pltpu.CompilerParams(collective_id=0, has_side_effects=True, **params),
        cost_estimate=pl.CostEstimate(
            flops=2 * n * CAP * 2 * tiles * QB * depth, bytes_accessed=10 ** 7, transcendentals=0),
    )(ids.T, prob.T, scale.transpose(1, 0, 2), tokens, gate_up)


def solution(mesh):
    n = mesh.shape["blk"]
    placed = (
        P(("groups", "blk"), None),
        P(("groups", "blk"), None),
        P(("groups", "blk"), None),
        P(None, "blk", None),
        P(None, "blk", None),
    )

    def body(tokens, expert_ids, route_prob, gate_up, block_scale):
        return local(n, expert_ids, route_prob, block_scale, tokens, gate_up)

    return jax.shard_map(
        body, mesh=mesh, in_specs=placed, out_specs=P(("groups", "blk"), None), check_vma=False
    )
```

time: 144 us -> 49.9 us (0.35)
  waiting for transfers between devices: 73.9 us -> 0 us
  Pallas kernels: 0 us -> 47.9 us
  starting transfers between devices: 27.1 us -> 0 us
  local copies, waits for them, and re-layouts: 26.4 us -> 1.77 us
  matrix products: 9.96 us -> 0 us
  other arithmetic: 5.75 us -> 0 us
    all_to_all x2 -> x0, waiting for transfers between devices: 73.9 us -> none  [the longest x1 56.7 us: local(): lax.all_to_all(outgoing, 'blk', split_axis=0, concat_axis=0, tiled=True)]
    pallas_call x0 -> x1, Pallas kernels: none -> 47.9 us  [local(): pl.pallas_call(functools.partial(kernel, n, parts), out_shape=jax.ShapeDt...]
    all_to_all x2 -> x0, starting transfers between devices: 27.1 us -> none  [the longest x1 19.6 us: local(): lax.all_to_all(hidden, 'blk', split_axis=0, concat_axis=2, tiled=True)]
    reshape x1 -> x0, local copies, waits for them, and re-layouts: 13.8 us -> none  [dequantize(): expanded = jnp.repeat(jnp.repeat(block_scale, QB, axis=1), QB, axis=2)]
    dot_general x1 -> x0, matrix products: 9.96 us -> none  [local(): jnp.einsum('scd,phd->psch', lax.all_to_all(outgoing, 'blk', split_axis=0,...]
    broadcast_in_dim x5 -> x0, local copies, waits for them, and re-layouts: 9.83 us -> none  [the longest x2 7.12 us: dequantize(): expanded = jnp.repeat(jnp.repeat(block_scale, QB, axis=1), QB, axis=2)]
    convert_element_type x1 -> x0, other arithmetic: 1.95 us -> none  [local(): return (share_columns * activation).astype(jnp.bfloat16)]
  transfers between devices with their start and end apart: 2 -> 0, of which waited for: 2 -> 0; matrix products, arithmetic and copies ran while one was open for 16% -> 0% of each run, Pallas kernels for 0% -> 0%
where the time goes in v2:
time: 49.9 us; the launch traced here: 49.7 us
  Pallas kernels  47.9 us (96%)
  local copies, waits for them, and re-layouts  1.77 us (4%)
    pallas_call x1, Pallas kernels, local(): pl.pallas_call(functools.partial(kernel, n, parts), out_shape=jax.ShapeDt...  47.9 us
    unnamed x1, local copies, waits for them, and re-layouts  1.77 us

profile of v2, /device:TPU:0, one launch (start us, length us, event | category | flops | bytes accessed | tf_op | source)
XLA Modules:
  0.0 49.7 jit_solution(12974707818779832369)
XLA Ops:
  0.0 47.9 %shard_map.55 = bf16[32,6144]{1,0:T(8,128)(2,1)} custom-call(s32[8,256]{1,0:T(8,128)} %bitcast.3, f32[8,256]{1,0:T(8,128)} %bitcast.4, f32[3,2,32]{2,1,0:T(2,128)} %bitcast.5, bf16[256,4096]{1,0:T(8,128)(2,1)} %tok_hbm.1, bf16[2,384,4096]{2,1,0:T(8,128)(2,1)} %w_hbm.1), custom_call_target="tpu_custom_call" | custom-call | flops 3221225472 | bytes 10000000 | tf_op jit(solution)/shard_map/pallas_call | solution.py:260
  47.9 1.8 %copy.7 = bf16[32,6144]{1,0:T(8,128)(2,1)} copy(bf16[32,6144]{1,0:T(8,128)(2,1)} %shard_map.55) | data formatting | bytes 786432

commit v3 on v2

--- a/solution.py
+++ b/solution.py
@@ -190,7 +190,7 @@
 
     for i in range(WINDOW):
         send_z(*order[i])
-        if i < 2:
+        if local_chunks:
             local_chunk()
     while todo:
         todo.pop(0)()
@@ -215,9 +215,7 @@
         arrived_y(s, h, c)
         left[s, h] -= 1
         if left[s, h] == 0:
-            if s == last:
-                queue(s, (h,))
-            elif left[s, 1 - h] == 0:
+            if left[s, 1 - h] == 0:
                 queue(s, (0, 1))
 
     for i, event in enumerate(order):

time: 49.9 us -> 47.8 us (0.958)
  Pallas kernels: 47.9 us -> 45.8 us
    pallas_call x1, Pallas kernels: 47.9 us -> 45.8 us  [local(): pl.pallas_call(functools.partial(kernel, n, parts), out_shape=jax.ShapeDt...]
where the time goes in v3:
time: 47.8 us; the launch traced here: 47.6 us
  Pallas kernels  45.8 us (96%)
  local copies, waits for them, and re-layouts  1.77 us (4%)
    pallas_call x1, Pallas kernels, local(): pl.pallas_call(functools.partial(kernel, n, parts), out_shape=jax.ShapeDt...  45.8 us
    unnamed x1, local copies, waits for them, and re-layouts  1.77 us

profile of v3, /device:TPU:0, one launch (start us, length us, event | category | flops | bytes accessed | tf_op | source)
XLA Modules:
  0.0 47.6 jit_solution(14222998456804540164)
XLA Ops:
  0.0 45.8 %shard_map.55 = bf16[32,6144]{1,0:T(8,128)(2,1)} custom-call(s32[8,256]{1,0:T(8,128)} %bitcast.3, f32[8,256]{1,0:T(8,128)} %bitcast.4, f32[3,2,32]{2,1,0:T(2,128)} %bitcast.5, bf16[256,4096]{1,0:T(8,128)(2,1)} %tok_hbm.1, bf16[2,384,4096]{2,1,0:T(8,128)(2,1)} %w_hbm.1), custom_call_target="tpu_custom_call" | custom-call | flops 3221225472 | bytes 10000000 | tf_op jit(solution)/shard_map/pallas_call | solution.py:258
  45.8 1.8 %copy.7 = bf16[32,6144]{1,0:T(8,128)(2,1)} copy(bf16[32,6144]{1,0:T(8,128)(2,1)} %shard_map.55) | data formatting | bytes 786432
